TPU v7x, 128 devices: a whole 4x4x4 slice. The times are simulated.
128 devices in a mesh: dp: 8 (over y, core), ctx: 16 (over z, x).
Axes of the slice: x: 4, y: 4, z: 4, core: 2. Of those that a mesh axis runs over, the one named last changes fastest.
Arguments:
- query_rows: bfloat16 [32768, 8, 128], P(('dp', 'ctx')), parts along dimension 0, may hold values from -17 to 17
- key_rows: bfloat16 [32768, 128], P(('dp', 'ctx')), parts along dimension 0, may hold values from -17 to 17
- value_rows: bfloat16 [32768, 128], P(('dp', 'ctx')), parts along dimension 0, may hold values from -1.5 to 1.5
- grad_out: bfloat16 [32768, 8, 128], P(('dp', 'ctx')), parts along dimension 0, may hold values from -6 to 6
Outputs:
- attended: bfloat16 [32768, 8, 128], P(('dp', 'ctx')), parts along dimension 0
- grad_query: float32 [32768, 8, 128], P(('dp', 'ctx')), parts along dimension 0
- grad_key: float32 [32768, 128], P(('dp', 'ctx')), parts along dimension 0
- grad_value: float32 [32768, 128], P(('dp', 'ctx')), parts along dimension 0
There are 8 independent parts, one for each index of `dp`. A program takes and returns all parts, laid end to end along the dimension named above; each array names one. Nothing has to cross between parts.
All inputs are finite; a program needn't handle non-finite values.
Results may differ from a plain program's by a relative error of at most 0.022.
Values may be sent and summed in bfloat16 or wider, within the bound.
No kernel may reach another device: no remote copies, remote signals or barrier semaphores. Data moves between devices by JAX's collectives and lax.ppermute only.
A program may use at most 64 MiB of HBM per device.

v0:
```python
import functools
import math

import jax
import jax.numpy as jnp
from jax import lax
from jax.experimental import pallas as pl
from jax.experimental.pallas import tpu as pltpu
from jax.sharding import PartitionSpec as P

f32 = jnp.float32
bf = jnp.bfloat16
NEG = -1e30
FWD = 1024
MIB = 18
V = pl.BlockSpec(memory_space=pltpu.VMEM)
S = pl.BlockSpec(memory_space=pltpu.SMEM)
COST = pl.CostEstimate(flops=1000, bytes_accessed=1000, transcendentals=0)
PARAMS = pltpu.CompilerParams(vmem_limit_bytes=MIB * 2**20)


def mm(a, b, ca, cb):
    return lax.dot_general(a, b, (((ca,), (cb,)), ((), ())), preferred_element_type=f32)


def sd(shape, dtype):
    return jax.ShapeDtypeStruct(shape, dtype)


def load_kernel(q, go, own, q_out, go_out):
    q_out[...] = q[...]
    go_out[...] = go[...]


def load(q, go, own):
    rows, hd = q.shape
    return pl.pallas_call(
        load_kernel,
        out_shape=(sd((rows, hd), bf), sd((rows, hd), bf)),
        in_specs=[V, V, pl.BlockSpec(memory_space=pl.ANY)],
        out_specs=(V, V),
        compiler_params=PARAMS,
        name="load",
        cost_estimate=COST,
    )(q, go, own)


def blocks_of(refs):
    found = []
    for ref in refs:
        found += [ref] if len(ref.shape) == 2 else [ref.at[j] for j in range(ref.shape[0])]
    return found


def each(count, diagonal, total, step):
    if diagonal:
        step(0, True)
        for j in range(1, total):
            pl.when(count > j)(functools.partial(step, j, False))
    else:

        @pl.when(count > 0)
        def _():
            for j in range(total):
                step(j, False)


def forward_kernel(heads, n_kv, first, last, cnt, q, go, *refs):
    refs = list(refs)
    kv = blocks_of(refs[:n_kv])
    refs = refs[n_kv:]
    if not first:
        stat_in, o_in = refs[:2]
        refs = refs[2:]
    p_all, stat = refs[:2]
    if last:
        att, final, o_t, s_all = refs[2:]
    else:
        o_t, s_all = refs[2:]
    rows, hd = q.shape
    blk = kv[0].shape[0]
    lg = hd**-0.5 * math.log2(math.e)
    count = cnt[0]
    width = min(FWD, rows)

    def put(c, j, masked):
        s = mm(kv[j][:, :hd], q[c, :], 1, 1) * lg
        if masked:
            u = lax.broadcasted_iota(jnp.int32, (blk, width), 0)
            t = (lax.broadcasted_iota(jnp.int32, (blk, width), 1) + c.start) // heads
            s = jnp.where(u <= t, s, NEG)
        s_all[j, :, c] = s
        return jnp.max(s.reshape(blk // 8, 8, width), axis=0)

    def weigh(c, j, top, total, out):
        p = jnp.exp2(s_all[j, :, c].reshape(blk // 8, 8, width) - top[None])
        total = total + jnp.sum(p, axis=0)
        p = p.reshape(blk, width).astype(bf)
        p_all[j, :, c] = p
        return total, out + mm(kv[j][:, hd:], p, 0, 0)

    def chunk(c, js):
        tops = [put(c, j, first and j == 0) for j in js]
        top = jnp.max(functools.reduce(jnp.maximum, tops), axis=0, keepdims=True)
        top = jnp.broadcast_to(top, (8, width))
        if not first:
            old = stat_in[0:8, c]
            top = jnp.maximum(old, top)
        total = jnp.zeros((8, width), f32)
        out = jnp.zeros((hd, width), f32)
        for j in js:
            total, out = weigh(c, j, top, total, out)
        if not first:
            shrink = jnp.exp2(old - top)
            total = total + stat_in[8:16, c] * shrink
            out = out + (o_in[:, c].reshape(hd // 8, 8, width) * shrink[None]).reshape(hd, width)
        stat[0:8, c] = top
        stat[8:16, c] = total
        o_t[:, c] = out

    def finish(c):
        total = jnp.sum(stat[8:16, c], axis=0, keepdims=True)
        share = jnp.broadcast_to(1.0 / total, (8, width))
        a_t = (o_t[:, c].reshape(hd // 8, 8, width) * share[None]).reshape(hd, width).astype(bf)
        att[:, c] = a_t
        dot = jnp.sum(a_t.astype(f32) * go[c, :].T.astype(f32), axis=0, keepdims=True)
        final[0:8, c] = stat[0:8, c] + jnp.broadcast_to(jnp.log2(total), (8, width))
        final[8:16, c] = jnp.broadcast_to(dot, (8, width))


    def over(step):
        @pl.loop(0, rows // width)
        def _(i):
            step(pl.ds(pl.multiple_of(i * width, width), width))

    if first:
        for m in range(1, len(kv) + 1):

            @pl.when(count == m)
            def _(m=m):
                over(lambda c: chunk(c, range(m)))
    else:

        @pl.when(count > 0)
        def _():
            over(lambda c: chunk(c, range(len(kv))))

        @pl.when(count == 0)
        def _():
            stat[...] = stat_in[...]
            o_t[...] = o_in[...]

    if last:
        over(finish)


def forward(cnt, q, go, kv, state, last, heads):
    rows, hd = q.shape
    blk = kv[0].shape[-2]
    nb = sum(1 if len(a.shape) == 2 else a.shape[0] for a in kv)
    first = state is None
    outs = [sd((nb, blk, rows), bf), sd((16, rows), f32)]
    outs += [sd((hd, rows), bf), sd((16, rows), f32)] if last else [sd((hd, rows), f32)]
    scratch = [pltpu.VMEM((hd, rows), f32)] if last else []
    return pl.pallas_call(
        functools.partial(forward_kernel, heads, len(kv), first, last),
        out_shape=tuple(outs),
        in_specs=[S] + [V] * (2 + len(kv) + (0 if first else 2)),
        out_specs=(V,) * len(outs),
        scratch_shapes=scratch + [pltpu.VMEM((nb, blk, rows), f32)],
        compiler_params=PARAMS,
        name="forward_last" if last else "forward_first" if first else "forward",
        cost_estimate=COST,
    )(cnt, q, go, *kv, *(state or ()))


def backward_kernel(n_kv, first, last, split, cnt, q, go, p_all, stat, final, *refs):
    refs = list(refs)
    kv = refs[0] if n_kv == 1 else refs[:n_kv]
    refs = refs[n_kv:]
    dq_in = None if first else refs.pop(0)
    nb, blk, rows = p_all.shape
    outs = [refs.pop(0) for _ in range(nb if split else 1)]
    dq_t = refs.pop(0)
    scale = refs.pop(0)
    dkv = refs.pop(0) if split else outs[0]
    hd = q.shape[1]
    root = hd**-0.5

    def block(j):
        return kv[j] if n_kv > 1 else kv.at[j]

    def piece(j):
        w = p_all[j].astype(f32).reshape(blk // 8, 8, rows) * scale[...][None]
        gp = mm(block(j)[:, hd:], go[...], 1, 1).reshape(blk // 8, 8, rows)
        gs = (w * (gp - final[8:16, :][None])).reshape(blk, rows).astype(bf)
        w = w.reshape(blk, rows).astype(bf)
        return mm(gs, q[...], 1, 0), mm(w, go[...], 1, 0), gs

    def back(js):
        found = [piece(j) for j in js]
        for j, (dk, dv, gs) in zip(js, found):
            dkv[j, :, :hd] = (dk * root).astype(bf)
            dkv[j, :, hd:] = dv.astype(bf)
        dq_t[...] += sum(mm(block(j)[:, :hd], gs, 0, 0) for j, (_, _, gs) in zip(js, found))

    dq_t[...] = jnp.zeros_like(dq_t) if first else dq_in[...]

    @pl.when(cnt[0] > 0)
    def _():
        scale[...] = jnp.exp2(stat[0:8, :] - final[0:8, :])

    pl.when(cnt[0] == nb)(functools.partial(back, range(nb)))
    @pl.when(cnt[0] < nb)
    def _():
        if last:
            @pl.loop(0, cnt[0])
            def _(j):
                back([j])

        @pl.loop(cnt[0], nb)
        def _(j):
            dkv[j] = jnp.zeros((blk, 2 * hd), bf)

    if split:
        for j in range(nb):
            outs[j][...] = dkv[j]


def backward(cnt, q, go, p_all, stat, final, kv, dq_t, last, split):
    rows, hd = q.shape
    nb, blk = p_all.shape[:2]
    first = dq_t is None
    outs = [sd((blk, 2 * hd), bf)] * nb if split else [sd((nb, blk, 2 * hd), bf)]
    outs += [sd((hd, rows), f32)]
    scratch = [pltpu.VMEM((8, rows), f32)]
    scratch += [pltpu.VMEM((nb, blk, 2 * hd), bf)] if split else []
    return pl.pallas_call(
        functools.partial(backward_kernel, len(kv), first, last, split),
        out_shape=tuple(outs),
        in_specs=[S] + [V] * (5 + len(kv) + (0 if first else 1)),
        out_specs=(V,) * len(outs),
        scratch_shapes=scratch,
        compiler_params=PARAMS,
        name="backward_last" if last else "backward",
        cost_estimate=COST,
    )(cnt, q, go, p_all, stat, final, *kv, *([] if first else [dq_t]))


def finish_kernel(att_t, dq_t, att, dq):
    att[...] = att_t[...].T
    dq[...] = (dq_t[...] * dq.shape[1] ** -0.5).T


def finish(att_t, dq_t):
    hd, rows = dq_t.shape
    return pl.pallas_call(
        finish_kernel,
        out_shape=(sd((rows, hd), bf), sd((rows, hd), f32)),
        in_specs=[V, V],
        out_specs=(V, V),
        compiler_params=PARAMS,
        name="finish",
        cost_estimate=COST,
    )(att_t, dq_t)


def per_device(query_rows, key_rows, value_rows, grad_out):
    me = lax.axis_index("ctx").astype(jnp.int32)
    n = lax.axis_size("ctx")
    side = math.isqrt(n)
    z, x = me // side, me % side
    blk, heads, hd = query_rows.shape
    q = query_rows.reshape(blk * heads, hd)
    go = grad_out.reshape(blk * heads, hd)

    def along_x(value, by):
        return lax.ppermute(value, "ctx", [(i, i // side * side + (i + by) % side) for i in range(n)])

    def along_z(value, by, wrap=True):
        pairs = [(i, (i + side * by) % n) for i in range(n)]
        if not wrap:
            pairs = [(i, j) for i, j in pairs if (j > i) == (by > 0)]
        return lax.ppermute(value, "ctx", pairs)

    own = lax.optimization_barrier(jnp.concatenate([key_rows, value_rows], axis=1))
    q, go = load(q, go, own)
    steps = range(1, side)
    far2 = along_z(own, 2)
    near = [along_x(own, r) for r in steps]
    far2, q, go, *near = lax.optimization_barrier((far2, q, go, *near))
    line = jnp.stack([own] + near)
    far1 = along_z(line, 1)
    far3 = along_z(line, 3)
    far2 = [far2] + [along_x(far2, r) for r in steps]
    count = {r: jnp.where(z >= r, side, 0).astype(jnp.int32).reshape(1) for r in steps}
    count[0] = (x + 1).reshape(1)
    kvs = {0: [line], 1: [far1], 3: [far3], 2: far2}
    p, top = {}, {}
    state = None
    for r in (0, 2, 1):
        p[r], *state = forward(count[r], q, go, kvs[r], state, False, heads)
        top[r] = state[0]
    p[3], top[3], att, final = forward(count[3], q, go, kvs[3], state, True, heads)

    def back(r, dq_t, last, split):
        return backward(count[r], q, go, p[r], top[r], final, kvs[r], dq_t, last, split)

    part3, dq_t = back(3, None, False, False)
    part3 = along_z(part3, -3, False)
    part1, dq_t = back(1, dq_t, False, False)
    part1 = along_z(part1, -1)
    *part2, dq_t = back(2, dq_t, False, True)
    part2 = [part2[0]] + [along_x(part2[r], -r) for r in steps]
    dq_t, part3 = lax.optimization_barrier((dq_t, part3))
    *part0, dq = back(0, dq_t, True, True)
    part2, part0 = lax.optimization_barrier((part2, part0))
    sum2 = sum(a.astype(f32) for a in part2).astype(bf)
    sum2 = along_z(sum2, -2, False)
    total = [part0[r].astype(f32) + part3[r].astype(f32) + part1[r].astype(f32) for r in range(side)]
    parts = [along_x(total[r].astype(bf), -r) for r in steps]
    att, dq = finish(att, dq)
    parts, att, dq, sum2 = lax.optimization_barrier((parts, att, dq, sum2))
    grads = total[0] + sum2.astype(f32)
    for part in parts:
        grads += part.astype(f32)
    return (att.reshape(blk, heads, hd), dq.reshape(blk, heads, hd), grads[:, :hd], grads[:, hd:])


def solution(mesh):
    rows3 = P(("dp", "ctx"), None, None)
    rows2 = P(("dp", "ctx"), None)
    return jax.shard_map(
        per_device,
        mesh=mesh,
        in_specs=(rows3, rows2, rows2, rows3),
        out_specs=(rows3, rows3, rows2, rows2),
        check_vma=False,
    )
```

profile of v0, /device:TPU:0, one launch (start us, length us, event | category | flops | bytes accessed | tf_op | source)
XLA Modules:
  0.0 69.7 jit_solution(17307338827694288405)
XLA Ops:
  0.6 0.9 %pad_maximum_fusion.1.own = bf16[256,256]{1,0:T(8,128)(2,1)S(1)} fusion(bf16[256,128]{1,0:T(8,128)(2,1)} %param.6, bf16[256,128]{1,0:T(8,128)(2,1)} %param.5), kind=kLoop, calls=%fused_computation.21 | loop fusion | flops 262144 | bytes 262144 | tf_op jit(solution)/shard_map/concatenate | solution.py:286
  1.5 2.9 %collective-permute-start.3 = (bf16[256,256]{1,0:T(8,128)(2,1)S(1)}, bf16[256,256]{1,0:T(8,128)(2,1)S(1)}, u32[]{:S(2)}, u32[]{:S(2)}) collective-permute-start(bf16[256,256]{1,0:T(8,128)(2,1)S(1)} %pad_maximum_fusion.1.own), channel_id=1, source_target_pairs={{0,3},{1,0},{2,1},{3,2},{4,7},{5,4},{6,5},{7,6},{8,11},{9,8},{10,9... | collective-permute-start | bytes 393224 | tf_op jit(solution)/shard_map/ppermute | solution.py:278
  4.4 0.8 %collective-permute-start.2 = (bf16[256,256]{1,0:T(8,128)(2,1)S(1)}, bf16[256,256]{1,0:T(8,128)(2,1)S(1)}, u32[]{:S(2)}, u32[]{:S(2)}) collective-permute-start(bf16[256,256]{1,0:T(8,128)(2,1)S(1)} %pad_maximum_fusion.1.own), channel_id=1, source_target_pairs={{0,2},{1,3},{2,0},{3,1},{4,6},{5,7},{6,4},{7,5},{8,10},{9,11},{10,... | collective-permute-start | bytes 393224 | tf_op jit(solution)/shard_map/ppermute | solution.py:278
  5.2 0.9 %collective-permute-start.1 = (bf16[256,256]{1,0:T(8,128)(2,1)S(1)}, bf16[256,256]{1,0:T(8,128)(2,1)S(1)}, u32[]{:S(2)}, u32[]{:S(2)}) collective-permute-start(bf16[256,256]{1,0:T(8,128)(2,1)S(1)} %pad_maximum_fusion.1.own), channel_id=1, source_target_pairs={{0,1},{1,2},{2,3},{3,0},{4,5},{5,6},{6,7},{7,4},{8,9},{9,10},{10,1... | collective-permute-start | bytes 393224 | tf_op jit(solution)/shard_map/ppermute | solution.py:278
  6.1 3.9 %collective-permute-start = (bf16[256,256]{1,0:T(8,128)(2,1)S(1)}, bf16[256,256]{1,0:T(8,128)(2,1)S(1)}, u32[]{:S(2)}, u32[]{:S(2)}) collective-permute-start(bf16[256,256]{1,0:T(8,128)(2,1)S(1)} %pad_maximum_fusion.1.own), channel_id=1, source_target_pairs={{0,8},{1,9},{2,10},{3,11},{4,12},{5,13},{6,14},{7,15},{8,0},{9,1},... | collective-permute-start | bytes 393224 | tf_op jit(solution)/shard_map/ppermute | solution.py:284
  10.0 1.0 %copy-done = bf16[256,8,128]{2,1,0:T(8,128)(2,1)S(1)} copy-done((bf16[256,8,128]{2,1,0:T(8,128)(2,1)S(1)}, bf16[256,8,128]{2,1,0:T(8,128)(2,1)}, u32[]{:S(2)}) %copy-start) | copy-done | bytes 524312
  11.0 1.0 %copy-done.1 = bf16[256,8,128]{2,1,0:T(8,128)(2,1)S(1)} copy-done((bf16[256,8,128]{2,1,0:T(8,128)(2,1)S(1)}, bf16[256,8,128]{2,1,0:T(8,128)(2,1)}, u32[]{:S(2)}) %copy-start.1) | copy-done | bytes 524312
  12.1 0.1 load.1
  12.2 0.0 collective-permute-done.3
  12.2 0.1 collective-permute-done.2
  12.3 1.4 %collective-permute-done.1 = bf16[256,256]{1,0:T(8,128)(2,1)S(1)} collective-permute-done((bf16[256,256]{1,0:T(8,128)(2,1)S(1)}, bf16[256,256]{1,0:T(8,128)(2,1)S(1)}, u32[]{:S(2)}, u32[]{:S(2)}) %collective-permute-start.1) | collective-permute-done | bytes 131104 | tf_op jit(solution)/shard_map/ppermute | solution.py:278
  13.7 0.1 pad_maximum_fusion.refs_0_
  13.8 2.0 %collective-permute-start.8 = (bf16[4,256,256]{2,1,0:T(8,128)(2,1)S(1)}, bf16[4,256,256]{2,1,0:T(8,128)(2,1)S(1)}, u32[]{:S(2)}, u32[]{:S(2)}) collective-permute-start(bf16[4,256,256]{2,1,0:T(8,128)(2,1)S(1)} %pad_maximum_fusion.refs_0_), channel_id=1, source_target_pairs={{0,4},{1,5},{2,6},{3,7},{4,8},{5,9},{6,10},{7,11},{8,12},{9,13},{1... | collective-permute-start | bytes 1572872 | tf_op jit(solution)/shard_map/ppermute | solution.py:284
  15.8 2.2 %collective-permute-start.7 = (bf16[4,256,256]{2,1,0:T(8,128)(2,1)S(1)}, bf16[4,256,256]{2,1,0:T(8,128)(2,1)S(1)}, u32[]{:S(2)}, u32[]{:S(2)}) collective-permute-start(bf16[4,256,256]{2,1,0:T(8,128)(2,1)S(1)} %pad_maximum_fusion.refs_0_), channel_id=1, source_target_pairs={{0,12},{1,13},{2,14},{3,15},{4,0},{5,1},{6,2},{7,3},{8,4},{9,5},{1... | collective-permute-start | bytes 1572872 | tf_op jit(solution)/shard_map/ppermute | solution.py:284
  18.0 1.2 %collective-permute-start.6 = (bf16[256,256]{1,0:T(8,128)(2,1)S(1)}, bf16[256,256]{1,0:T(8,128)(2,1)S(1)}, u32[]{:S(2)}, u32[]{:S(2)}) collective-permute-start(bf16[256,256]{1,0:T(8,128)(2,1)S(1)} %collective-permute-done.refs_0_), channel_id=1, source_target_pairs={{0,3},{1,0},{2,1},{3,2},{4,7},{5,4},{6,5},{7,6},{8,11},{9,8},{10,9... | collective-permute-start | bytes 393224 | tf_op jit(solution)/shard_map/ppermute | solution.py:278
  19.2 1.5 %collective-permute-start.5 = (bf16[256,256]{1,0:T(8,128)(2,1)S(1)}, bf16[256,256]{1,0:T(8,128)(2,1)S(1)}, u32[]{:S(2)}, u32[]{:S(2)}) collective-permute-start(bf16[256,256]{1,0:T(8,128)(2,1)S(1)} %collective-permute-done.refs_0_), channel_id=1, source_target_pairs={{0,2},{1,3},{2,0},{3,1},{4,6},{5,7},{6,4},{7,5},{8,10},{9,11},{10,... | collective-permute-start | bytes 393224 | tf_op jit(solution)/shard_map/ppermute | solution.py:278
  20.7 1.3 %forward_first.1 = (bf16[4,256,2048]{2,1,0:T(8,128)(2,1)S(1)}, f32[16,2048]{1,0:T(8,128)S(1)}, f32[128,2048]{1,0:T(8,128)S(1)}) custom-call(s32[1]{0:T(128)} %bitcast.3.cnt, bf16[2048,128]{1,0:T(8,128)(2,1)S(1)} %get-tuple-element.59.q, bf16[2048,128]{1,0:T(8,128)(2,1)S(1)} %get-tuple-element.60.go, bf16[4,256,256]{2,1,0:T(8,128)(2,1)S(1)} %pad_maximum_fusion.refs_0_), custom_call_target="tpu_custom_call" | custom-call | flops 1000 | bytes 1000 | tf_op jit(solution)/shard_map/forward_first/pallas_call | solution.py:165
  22.1 2.3 %collective-permute-done.6.refs_3_ = bf16[256,256]{1,0:T(8,128)(2,1)S(1)} collective-permute-done((bf16[256,256]{1,0:T(8,128)(2,1)S(1)}, bf16[256,256]{1,0:T(8,128)(2,1)S(1)}, u32[]{:S(2)}, u32[]{:S(2)}) %collective-permute-start.6) | collective-permute-done | bytes 131104 | tf_op jit(solution)/shard_map/ppermute | solution.py:278
  24.3 2.2 %collective-permute-done.5.refs_2_ = bf16[256,256]{1,0:T(8,128)(2,1)S(1)} collective-permute-done((bf16[256,256]{1,0:T(8,128)(2,1)S(1)}, bf16[256,256]{1,0:T(8,128)(2,1)S(1)}, u32[]{:S(2)}, u32[]{:S(2)}) %collective-permute-start.5) | collective-permute-done | bytes 131104 | tf_op jit(solution)/shard_map/ppermute | solution.py:278
  26.6 1.1 %collective-permute-done.4.refs_1_ = bf16[256,256]{1,0:T(8,128)(2,1)S(1)} collective-permute-done((bf16[256,256]{1,0:T(8,128)(2,1)S(1)}, bf16[256,256]{1,0:T(8,128)(2,1)S(1)}, u32[]{:S(2)}, u32[]{:S(2)}) %collective-permute-start.4) | collective-permute-done | bytes 131104 | tf_op jit(solution)/shard_map/ppermute | solution.py:278
  27.7 0.1 forward.2
  27.7 2.1 %collective-permute-done.8.refs_0_ = bf16[4,256,256]{2,1,0:T(8,128)(2,1)S(1)} collective-permute-done((bf16[4,256,256]{2,1,0:T(8,128)(2,1)S(1)}, bf16[4,256,256]{2,1,0:T(8,128)(2,1)S(1)}, u32[]{:S(2)}, u32[]{:S(2)}) %collective-permute-start.8) | collective-permute-done | bytes 524320 | tf_op jit(solution)/shard_map/ppermute | solution.py:284
  29.8 0.1 forward.3
  29.9 0.4 forward_last.1
  30.3 0.3 backward.3
  30.6 1.3 %collective-permute-start.12 = (bf16[4,256,256]{2,1,0:T(8,128)(2,1)S(1)}, bf16[4,256,256]{2,1,0:T(8,128)(2,1)S(1)}, u32[]{:S(2)}, u32[]{:S(2)}) collective-permute-start(bf16[4,256,256]{2,1,0:T(8,128)(2,1)S(1)} %get-tuple-element.84), channel_id=1, source_target_pairs={{12,0},{13,1},{14,2},{15,3},{28,16},{29,17},{30,18},{31,19},{44,32... | collective-permute-start | bytes 1572872 | tf_op jit(solution)/shard_map/ppermute | solution.py:284
  31.9 0.1 backward.4
  32.1 17.9 %collective-permute-start.13 = (bf16[4,256,256]{2,1,0:T(8,128)(2,1)S(1)}, bf16[4,256,256]{2,1,0:T(8,128)(2,1)S(1)}, u32[]{:S(2)}, u32[]{:S(2)}) collective-permute-start(bf16[4,256,256]{2,1,0:T(8,128)(2,1)S(1)} %get-tuple-element.92), channel_id=1, source_target_pairs={{0,12},{1,13},{2,14},{3,15},{4,0},{5,1},{6,2},{7,3},{8,4},{9,5},{1... | collective-permute-start | bytes 1572872 | tf_op jit(solution)/shard_map/ppermute | solution.py:284
  49.9 0.4 backward.5
  50.3 0.6 collective-permute-start.9
  51.0 1.0 %collective-permute-start.10 = (bf16[256,256]{1,0:T(8,128)(2,1)S(1)}, bf16[256,256]{1,0:T(8,128)(2,1)S(1)}, u32[]{:S(2)}, u32[]{:S(2)}) collective-permute-start(bf16[256,256]{1,0:T(8,128)(2,1)S(1)} %get-tuple-element.80), channel_id=1, source_target_pairs={{0,2},{1,3},{2,0},{3,1},{4,6},{5,7},{6,4},{7,5},{8,10},{9,11},{10,... | collective-permute-start | bytes 393224 | tf_op jit(solution)/shard_map/ppermute | solution.py:278
  51.9 0.9 %collective-permute-start.11 = (bf16[256,256]{1,0:T(8,128)(2,1)S(1)}, bf16[256,256]{1,0:T(8,128)(2,1)S(1)}, u32[]{:S(2)}, u32[]{:S(2)}) collective-permute-start(bf16[256,256]{1,0:T(8,128)(2,1)S(1)} %get-tuple-element.81), channel_id=1, source_target_pairs={{0,1},{1,2},{2,3},{3,0},{4,5},{5,6},{6,7},{7,4},{8,9},{9,10},{10,1... | collective-permute-start | bytes 393224 | tf_op jit(solution)/shard_map/ppermute | solution.py:278
  52.8 2.3 %collective-permute-done.12 = bf16[4,256,256]{2,1,0:T(8,128)(2,1)S(1)} collective-permute-done((bf16[4,256,256]{2,1,0:T(8,128)(2,1)S(1)}, bf16[4,256,256]{2,1,0:T(8,128)(2,1)S(1)}, u32[]{:S(2)}, u32[]{:S(2)}) %collective-permute-start.12) | collective-permute-done | bytes 524320 | tf_op jit(solution)/shard_map/ppermute | solution.py:284
  55.1 1.4 %backward_last.1 = (bf16[256,256]{1,0:T(8,128)(2,1)S(1)}, bf16[256,256]{1,0:T(8,128)(2,1)S(1)}, bf16[256,256]{1,0:T(8,128)(2,1)S(1)}, bf16[256,256]{1,0:T(8,128)(2,1)S(1)}, f32[128,2048]{1,0:T(8,128)S(1)}) custom-call(s32[1]{0:T(128)} %bitcast.3.cnt, bf16[2048,128]{1,0:T(8,128)(2,1)S(1)} %get-tuple-element.59.q, bf16[2048,128]{1,0:T(8,128)(2,1)S(1)} %get-tuple-element.60.go, ...), custom_call_target="tpu_custom_call" | custom-call | flops 1000 | bytes 1000 | tf_op jit(solution)/shard_map/backward_last/pallas_call | solution.py:238
  56.6 1.0 %collective-permute-done.10 = bf16[256,256]{1,0:T(8,128)(2,1)S(1)} collective-permute-done((bf16[256,256]{1,0:T(8,128)(2,1)S(1)}, bf16[256,256]{1,0:T(8,128)(2,1)S(1)}, u32[]{:S(2)}, u32[]{:S(2)}) %collective-permute-start.10) | collective-permute-done | bytes 131104 | tf_op jit(solution)/shard_map/ppermute | solution.py:278
  57.5 1.3 %collective-permute-done.11 = bf16[256,256]{1,0:T(8,128)(2,1)S(1)} collective-permute-done((bf16[256,256]{1,0:T(8,128)(2,1)S(1)}, bf16[256,256]{1,0:T(8,128)(2,1)S(1)}, u32[]{:S(2)}, u32[]{:S(2)}) %collective-permute-start.11) | collective-permute-done | bytes 131104 | tf_op jit(solution)/shard_map/ppermute | solution.py:278
  58.8 0.1 add_convert_fusion
  58.9 1.3 %collective-permute-start.17 = (bf16[256,256]{1,0:T(8,128)(2,1)S(1)}, bf16[256,256]{1,0:T(8,128)(2,1)S(1)}, u32[]{:S(2)}, u32[]{:S(2)}) collective-permute-start(bf16[256,256]{1,0:T(8,128)(2,1)S(1)} %add_convert_fusion), channel_id=1, source_target_pairs={{8,0},{9,1},{10,2},{11,3},{12,4},{13,5},{14,6},{15,7},{24,16},{25,... | collective-permute-start | bytes 393224 | tf_op jit(solution)/shard_map/ppermute | solution.py:284
  60.2 0.2 fusion.4
  60.4 0.1 collective-permute-start.16
  60.5 3.1 %collective-permute-start.15 = (bf16[256,256]{1,0:T(8,128)(2,1)S(1)}, bf16[256,256]{1,0:T(8,128)(2,1)S(1)}, u32[]{:S(2)}, u32[]{:S(2)}) collective-permute-start(bf16[256,256]{1,0:T(8,128)(2,1)S(1)} %get-tuple-element.111), channel_id=1, source_target_pairs={{0,2},{1,3},{2,0},{3,1},{4,6},{5,7},{6,4},{7,5},{8,10},{9,11},{10,... | collective-permute-start | bytes 393224 | tf_op jit(solution)/shard_map/ppermute | solution.py:278
  63.6 1.1 %collective-permute-start.14 = (bf16[256,256]{1,0:T(8,128)(2,1)S(1)}, bf16[256,256]{1,0:T(8,128)(2,1)S(1)}, u32[]{:S(2)}, u32[]{:S(2)}) collective-permute-start(bf16[256,256]{1,0:T(8,128)(2,1)S(1)} %get-tuple-element.112), channel_id=1, source_target_pairs={{0,3},{1,0},{2,1},{3,2},{4,7},{5,4},{6,5},{7,6},{8,11},{9,8},{10,9... | collective-permute-start | bytes 393224 | tf_op jit(solution)/shard_map/ppermute | solution.py:278
  64.7 1.4 %finish.1 = (bf16[2048,128]{1,0:T(8,128)(2,1)}, f32[2048,128]{1,0:T(8,128)}) custom-call(bf16[128,2048]{1,0:T(8,128)(2,1)S(1)} %get-tuple-element.95.att_t, f32[128,2048]{1,0:T(8,128)S(1)} %get-tuple-element.96.dq_t), custom_call_target="tpu_custom_call" | custom-call | flops 1000 | bytes 1000 | tf_op jit(solution)/shard_map/finish/pallas_call | solution.py:257
  66.1 1.1 %collective-permute-done.17 = bf16[256,256]{1,0:T(8,128)(2,1)S(1)} collective-permute-done((bf16[256,256]{1,0:T(8,128)(2,1)S(1)}, bf16[256,256]{1,0:T(8,128)(2,1)S(1)}, u32[]{:S(2)}, u32[]{:S(2)}) %collective-permute-start.17) | collective-permute-done | bytes 131104 | tf_op jit(solution)/shard_map/ppermute | solution.py:284
  67.3 0.8 %collective-permute-done.15 = bf16[256,256]{1,0:T(8,128)(2,1)S(1)} collective-permute-done((bf16[256,256]{1,0:T(8,128)(2,1)S(1)}, bf16[256,256]{1,0:T(8,128)(2,1)S(1)}, u32[]{:S(2)}, u32[]{:S(2)}) %collective-permute-start.15) | collective-permute-done | bytes 131104 | tf_op jit(solution)/shard_map/ppermute | solution.py:278
  68.0 0.9 %collective-permute-done.14 = bf16[256,256]{1,0:T(8,128)(2,1)S(1)} collective-permute-done((bf16[256,256]{1,0:T(8,128)(2,1)S(1)}, bf16[256,256]{1,0:T(8,128)(2,1)S(1)}, u32[]{:S(2)}, u32[]{:S(2)}) %collective-permute-start.14) | collective-permute-done | bytes 131104 | tf_op jit(solution)/shard_map/ppermute | solution.py:278
  68.9 0.1 fusion.3
  69.0 0.7 %fusion.7 = (f32[256,128]{1,0:T(8,128)}, f32[256,128]{1,0:T(8,128)}) fusion(f32[256,256]{1,0:T(8,128)S(1)} %fusion.3), kind=kLoop, calls=%fused_computation.22 | loop fusion | bytes 524288 | tf_op jit(solution)/shard_map/slice | solution.py:327
  (8 shorter events, 0.0 us)
Async XLA Ops:
  1.5 10.6 %collective-permute-start.3 = (bf16[256,256]{1,0:T(8,128)(2,1)S(1)}, bf16[256,256]{1,0:T(8,128)(2,1)S(1)}, u32[]{:S(2)}, u32[]{:S(2)}) collective-permute-start(bf16[256,256]{1,0:T(8,128)(2,1)S(1)} %pad_maximum_fusion.1.own), channel_id=1, source_target_pairs={{0,3},{1,0},{2,1},{3,2},{4,7},{5,4},{6,5},{7,6},{8,11},{9,8},{10,9... | collective-permute-start | bytes 393224 | tf_op jit(solution)/shard_map/ppermute | solution.py:278
  4.4 7.9 %collective-permute-start.2 = (bf16[256,256]{1,0:T(8,128)(2,1)S(1)}, bf16[256,256]{1,0:T(8,128)(2,1)S(1)}, u32[]{:S(2)}, u32[]{:S(2)}) collective-permute-start(bf16[256,256]{1,0:T(8,128)(2,1)S(1)} %pad_maximum_fusion.1.own), channel_id=1, source_target_pairs={{0,2},{1,3},{2,0},{3,1},{4,6},{5,7},{6,4},{7,5},{8,10},{9,11},{10,... | collective-permute-start | bytes 393224 | tf_op jit(solution)/shard_map/ppermute | solution.py:278
  5.2 8.5 %collective-permute-start.1 = (bf16[256,256]{1,0:T(8,128)(2,1)S(1)}, bf16[256,256]{1,0:T(8,128)(2,1)S(1)}, u32[]{:S(2)}, u32[]{:S(2)}) collective-permute-start(bf16[256,256]{1,0:T(8,128)(2,1)S(1)} %pad_maximum_fusion.1.own), channel_id=1, source_target_pairs={{0,1},{1,2},{2,3},{3,0},{4,5},{5,6},{6,7},{7,4},{8,9},{9,10},{10,1... | collective-permute-start | bytes 393224 | tf_op jit(solution)/shard_map/ppermute | solution.py:278
  6.1 7.6 %collective-permute-start = (bf16[256,256]{1,0:T(8,128)(2,1)S(1)}, bf16[256,256]{1,0:T(8,128)(2,1)S(1)}, u32[]{:S(2)}, u32[]{:S(2)}) collective-permute-start(bf16[256,256]{1,0:T(8,128)(2,1)S(1)} %pad_maximum_fusion.1.own), channel_id=1, source_target_pairs={{0,8},{1,9},{2,10},{3,11},{4,12},{5,13},{6,14},{7,15},{8,0},{9,1},... | collective-permute-start | bytes 393224 | tf_op jit(solution)/shard_map/ppermute | solution.py:284
  10.0 1.0 %copy-start = (bf16[256,8,128]{2,1,0:T(8,128)(2,1)S(1)}, bf16[256,8,128]{2,1,0:T(8,128)(2,1)}, u32[]{:S(2)}) copy-start(bf16[256,8,128]{2,1,0:T(8,128)(2,1)} %param.4) | copy-start | bytes 1572868
  11.0 1.0 %copy-start.1 = (bf16[256,8,128]{2,1,0:T(8,128)(2,1)S(1)}, bf16[256,8,128]{2,1,0:T(8,128)(2,1)}, u32[]{:S(2)}) copy-start(bf16[256,8,128]{2,1,0:T(8,128)(2,1)} %param.7) | copy-start | bytes 1572868
  13.8 16.0 %collective-permute-start.8 = (bf16[4,256,256]{2,1,0:T(8,128)(2,1)S(1)}, bf16[4,256,256]{2,1,0:T(8,128)(2,1)S(1)}, u32[]{:S(2)}, u32[]{:S(2)}) collective-permute-start(bf16[4,256,256]{2,1,0:T(8,128)(2,1)S(1)} %pad_maximum_fusion.refs_0_), channel_id=1, source_target_pairs={{0,4},{1,5},{2,6},{3,7},{4,8},{5,9},{6,10},{7,11},{8,12},{9,13},{1... | collective-permute-start | bytes 1572872 | tf_op jit(solution)/shard_map/ppermute | solution.py:284
  15.8 14.1 %collective-permute-start.7 = (bf16[4,256,256]{2,1,0:T(8,128)(2,1)S(1)}, bf16[4,256,256]{2,1,0:T(8,128)(2,1)S(1)}, u32[]{:S(2)}, u32[]{:S(2)}) collective-permute-start(bf16[4,256,256]{2,1,0:T(8,128)(2,1)S(1)} %pad_maximum_fusion.refs_0_), channel_id=1, source_target_pairs={{0,12},{1,13},{2,14},{3,15},{4,0},{5,1},{6,2},{7,3},{8,4},{9,5},{1... | collective-permute-start | bytes 1572872 | tf_op jit(solution)/shard_map/ppermute | solution.py:284
  18.0 6.4 %collective-permute-start.6 = (bf16[256,256]{1,0:T(8,128)(2,1)S(1)}, bf16[256,256]{1,0:T(8,128)(2,1)S(1)}, u32[]{:S(2)}, u32[]{:S(2)}) collective-permute-start(bf16[256,256]{1,0:T(8,128)(2,1)S(1)} %collective-permute-done.refs_0_), channel_id=1, source_target_pairs={{0,3},{1,0},{2,1},{3,2},{4,7},{5,4},{6,5},{7,6},{8,11},{9,8},{10,9... | collective-permute-start | bytes 393224 | tf_op jit(solution)/shard_map/ppermute | solution.py:278
  19.2 7.3 %collective-permute-start.5 = (bf16[256,256]{1,0:T(8,128)(2,1)S(1)}, bf16[256,256]{1,0:T(8,128)(2,1)S(1)}, u32[]{:S(2)}, u32[]{:S(2)}) collective-permute-start(bf16[256,256]{1,0:T(8,128)(2,1)S(1)} %collective-permute-done.refs_0_), channel_id=1, source_target_pairs={{0,2},{1,3},{2,0},{3,1},{4,6},{5,7},{6,4},{7,5},{8,10},{9,11},{10,... | collective-permute-start | bytes 393224 | tf_op jit(solution)/shard_map/ppermute | solution.py:278
  20.7 6.9 %collective-permute-start.4 = (bf16[256,256]{1,0:T(8,128)(2,1)S(1)}, bf16[256,256]{1,0:T(8,128)(2,1)S(1)}, u32[]{:S(2)}, u32[]{:S(2)}) collective-permute-start(bf16[256,256]{1,0:T(8,128)(2,1)S(1)} %collective-permute-done.refs_0_), channel_id=1, source_target_pairs={{0,1},{1,2},{2,3},{3,0},{4,5},{5,6},{6,7},{7,4},{8,9},{9,10},{10,1... | collective-permute-start | bytes 393224 | tf_op jit(solution)/shard_map/ppermute | solution.py:278
  30.6 24.5 %collective-permute-start.12 = (bf16[4,256,256]{2,1,0:T(8,128)(2,1)S(1)}, bf16[4,256,256]{2,1,0:T(8,128)(2,1)S(1)}, u32[]{:S(2)}, u32[]{:S(2)}) collective-permute-start(bf16[4,256,256]{2,1,0:T(8,128)(2,1)S(1)} %get-tuple-element.84), channel_id=1, source_target_pairs={{12,0},{13,1},{14,2},{15,3},{28,16},{29,17},{30,18},{31,19},{44,32... | collective-permute-start | bytes 1572872 | tf_op jit(solution)/shard_map/ppermute | solution.py:284
  32.1 28.1 %collective-permute-start.13 = (bf16[4,256,256]{2,1,0:T(8,128)(2,1)S(1)}, bf16[4,256,256]{2,1,0:T(8,128)(2,1)S(1)}, u32[]{:S(2)}, u32[]{:S(2)}) collective-permute-start(bf16[4,256,256]{2,1,0:T(8,128)(2,1)S(1)} %get-tuple-element.92), channel_id=1, source_target_pairs={{0,12},{1,13},{2,14},{3,15},{4,0},{5,1},{6,2},{7,3},{8,4},{9,5},{1... | collective-permute-start | bytes 1572872 | tf_op jit(solution)/shard_map/ppermute | solution.py:284
  50.3 6.2 %collective-permute-start.9 = (bf16[256,256]{1,0:T(8,128)(2,1)S(1)}, bf16[256,256]{1,0:T(8,128)(2,1)S(1)}, u32[]{:S(2)}, u32[]{:S(2)}) collective-permute-start(bf16[256,256]{1,0:T(8,128)(2,1)S(1)} %get-tuple-element.79), channel_id=1, source_target_pairs={{0,3},{1,0},{2,1},{3,2},{4,7},{5,4},{6,5},{7,6},{8,11},{9,8},{10,9... | collective-permute-start | bytes 393224 | tf_op jit(solution)/shard_map/ppermute | solution.py:278
  51.0 6.5 %collective-permute-start.10 = (bf16[256,256]{1,0:T(8,128)(2,1)S(1)}, bf16[256,256]{1,0:T(8,128)(2,1)S(1)}, u32[]{:S(2)}, u32[]{:S(2)}) collective-permute-start(bf16[256,256]{1,0:T(8,128)(2,1)S(1)} %get-tuple-element.80), channel_id=1, source_target_pairs={{0,2},{1,3},{2,0},{3,1},{4,6},{5,7},{6,4},{7,5},{8,10},{9,11},{10,... | collective-permute-start | bytes 393224 | tf_op jit(solution)/shard_map/ppermute | solution.py:278
  51.9 6.9 %collective-permute-start.11 = (bf16[256,256]{1,0:T(8,128)(2,1)S(1)}, bf16[256,256]{1,0:T(8,128)(2,1)S(1)}, u32[]{:S(2)}, u32[]{:S(2)}) collective-permute-start(bf16[256,256]{1,0:T(8,128)(2,1)S(1)} %get-tuple-element.81), channel_id=1, source_target_pairs={{0,1},{1,2},{2,3},{3,0},{4,5},{5,6},{6,7},{7,4},{8,9},{9,10},{10,1... | collective-permute-start | bytes 393224 | tf_op jit(solution)/shard_map/ppermute | solution.py:278
  58.9 8.4 %collective-permute-start.17 = (bf16[256,256]{1,0:T(8,128)(2,1)S(1)}, bf16[256,256]{1,0:T(8,128)(2,1)S(1)}, u32[]{:S(2)}, u32[]{:S(2)}) collective-permute-start(bf16[256,256]{1,0:T(8,128)(2,1)S(1)} %add_convert_fusion), channel_id=1, source_target_pairs={{8,0},{9,1},{10,2},{11,3},{12,4},{13,5},{14,6},{15,7},{24,16},{25,... | collective-permute-start | bytes 393224 | tf_op jit(solution)/shard_map/ppermute | solution.py:284
  60.4 6.9 %collective-permute-start.16 = (bf16[256,256]{1,0:T(8,128)(2,1)S(1)}, bf16[256,256]{1,0:T(8,128)(2,1)S(1)}, u32[]{:S(2)}, u32[]{:S(2)}) collective-permute-start(bf16[256,256]{1,0:T(8,128)(2,1)S(1)} %get-tuple-element.110), channel_id=1, source_target_pairs={{0,1},{1,2},{2,3},{3,0},{4,5},{5,6},{6,7},{7,4},{8,9},{9,10},{10,1... | collective-permute-start | bytes 393224 | tf_op jit(solution)/shard_map/ppermute | solution.py:278
  60.5 7.5 %collective-permute-start.15 = (bf16[256,256]{1,0:T(8,128)(2,1)S(1)}, bf16[256,256]{1,0:T(8,128)(2,1)S(1)}, u32[]{:S(2)}, u32[]{:S(2)}) collective-permute-start(bf16[256,256]{1,0:T(8,128)(2,1)S(1)} %get-tuple-element.111), channel_id=1, source_target_pairs={{0,2},{1,3},{2,0},{3,1},{4,6},{5,7},{6,4},{7,5},{8,10},{9,11},{10,... | collective-permute-start | bytes 393224 | tf_op jit(solution)/shard_map/ppermute | solution.py:278
  63.6 5.3 %collective-permute-start.14 = (bf16[256,256]{1,0:T(8,128)(2,1)S(1)}, bf16[256,256]{1,0:T(8,128)(2,1)S(1)}, u32[]{:S(2)}, u32[]{:S(2)}) collective-permute-start(bf16[256,256]{1,0:T(8,128)(2,1)S(1)} %get-tuple-element.112), channel_id=1, source_target_pairs={{0,3},{1,0},{2,1},{3,2},{4,7},{5,4},{6,5},{7,6},{8,11},{9,8},{10,9... | collective-permute-start | bytes 393224 | tf_op jit(solution)/shard_map/ppermute | solution.py:278
where the time goes:
time: 70.4 us; the launch traced here: 69.7 us
  starting transfers between devices  42.7 us (61%)
  waiting for transfers between devices  16.6 us (24%)
  Pallas kernels  5.63 us (8%)
  local copies, waits for them, and re-layouts  2.8 us (4%)
  other arithmetic  1.31 us (2%)
  between operations  0.77 us (1%)
    ppermute x6, starting transfers between devices, along_z(): return lax.ppermute(value, 'ctx', pairs)  28.5 us
    ppermute x12, starting transfers between devices, along_x(): lax.ppermute(value, 'ctx', [(i, i // side * side + (i + by) % side) for i...  14.1 us
    ppermute x12, waiting for transfers between devices, along_x(): lax.ppermute(value, 'ctx', [(i, i // side * side + (i + by) % side) for i...  11 us
    ppermute x6, waiting for transfers between devices, along_z(): return lax.ppermute(value, 'ctx', pairs)  5.53 us
    pallas_call x4, Pallas kernels, backward(): pl.pallas_call(functools.partial(backward_kernel, len(kv), first, last, s...  2.22 us
    unnamed x4, local copies, waits for them, and re-layouts  2.08 us
    pallas_call x4, Pallas kernels, forward(): pl.pallas_call(functools.partial(forward_kernel, heads, len(kv), first, l...  1.9 us
    pallas_call x1, Pallas kernels, finish(): pl.pallas_call(finish_kernel, out_shape=(sd((rows, hd), bf), sd((rows, hd...  1.45 us
  transfers between devices with their start and end apart: 18, of which 12 were waited for; matrix products, arithmetic and copies ran while one was open for 0% of the time, Pallas kernels for 7%

commit v1 on v0

--- a/solution.py
+++ b/solution.py
@@ -298,10 +298,10 @@
     kvs = {0: [line], 1: [far1], 3: [far3], 2: far2}
     p, top = {}, {}
     state = None
-    for r in (0, 2, 1):
+    for r in (0, 2, 3):
         p[r], *state = forward(count[r], q, go, kvs[r], state, False, heads)
         top[r] = state[0]
-    p[3], top[3], att, final = forward(count[3], q, go, kvs[3], state, True, heads)
+    p[1], top[1], att, final = forward(count[1], q, go, kvs[1], state, True, heads)
 
     def back(r, dq_t, last, split):
         return backward(count[r], q, go, p[r], top[r], final, kvs[r], dq_t, last, split)

time: 70.4 us -> 71.6 us (1.017)
  waiting for transfers between devices: 16.6 us -> 19 us
  starting transfers between devices: 42.7 us -> 41.5 us
    ppermute x6, waiting for transfers between devices: 5.53 us -> 7.94 us  [along_z(): return lax.ppermute(value, 'ctx', pairs)]
    ppermute x6, starting transfers between devices: 28.5 us -> 27.1 us  [along_z(): return lax.ppermute(value, 'ctx', pairs)]
  transfers between devices with their start and end apart: 18 -> 18, of which waited for: 12 -> 13; matrix products, arithmetic and copies ran while one was open for 0% -> 0% of each run, Pallas kernels for 7% -> 7%
where the time goes in v1:
time: 71.6 us; the launch traced here: 70.9 us
  starting transfers between devices  41.5 us (58%)
  waiting for transfers between devices  19 us (27%)
  Pallas kernels  5.62 us (8%)
  local copies, waits for them, and re-layouts  2.8 us (4%)
  other arithmetic  1.31 us (2%)
  between operations  0.77 us (1%)
    ppermute x6, starting transfers between devices, along_z(): return lax.ppermute(value, 'ctx', pairs)  27.1 us
    ppermute x12, starting transfers between devices, along_x(): lax.ppermute(value, 'ctx', [(i, i // side * side + (i + by) % side) for i...  14.4 us
    ppermute x12, waiting for transfers between devices, along_x(): lax.ppermute(value, 'ctx', [(i, i // side * side + (i + by) % side) for i...  11 us
    ppermute x6, waiting for transfers between devices, along_z(): return lax.ppermute(value, 'ctx', pairs)  7.94 us
    pallas_call x4, Pallas kernels, backward(): pl.pallas_call(functools.partial(backward_kernel, len(kv), first, last, s...  2.22 us
    unnamed x4, local copies, waits for them, and re-layouts  2.08 us
    pallas_call x4, Pallas kernels, forward(): pl.pallas_call(functools.partial(forward_kernel, heads, len(kv), first, l...  1.89 us
    pallas_call x1, Pallas kernels, finish(): pl.pallas_call(finish_kernel, out_shape=(sd((rows, hd), bf), sd((rows, hd...  1.45 us
  transfers between devices with their start and end apart: 18, of which 13 were waited for; matrix products, arithmetic and copies ran while one was open for 0% of the time, Pallas kernels for 7%

profile of v1, /device:TPU:0, one launch (start us, length us, event | category | flops | bytes accessed | tf_op | source)
XLA Modules:
  0.0 70.9 jit_solution(16985615034030377249)
XLA Ops:
  0.6 0.9 %pad_maximum_fusion.1.own = bf16[256,256]{1,0:T(8,128)(2,1)S(1)} fusion(bf16[256,128]{1,0:T(8,128)(2,1)} %param.6, bf16[256,128]{1,0:T(8,128)(2,1)} %param.5), kind=kLoop, calls=%fused_computation.21 | loop fusion | flops 262144 | bytes 262144 | tf_op jit(solution)/shard_map/concatenate | solution.py:286
  1.5 2.9 %collective-permute-start.3 = (bf16[256,256]{1,0:T(8,128)(2,1)S(1)}, bf16[256,256]{1,0:T(8,128)(2,1)S(1)}, u32[]{:S(2)}, u32[]{:S(2)}) collective-permute-start(bf16[256,256]{1,0:T(8,128)(2,1)S(1)} %pad_maximum_fusion.1.own), channel_id=1, source_target_pairs={{0,3},{1,0},{2,1},{3,2},{4,7},{5,4},{6,5},{7,6},{8,11},{9,8},{10,9... | collective-permute-start | bytes 393224 | tf_op jit(solution)/shard_map/ppermute | solution.py:278
  4.4 0.8 %collective-permute-start.2 = (bf16[256,256]{1,0:T(8,128)(2,1)S(1)}, bf16[256,256]{1,0:T(8,128)(2,1)S(1)}, u32[]{:S(2)}, u32[]{:S(2)}) collective-permute-start(bf16[256,256]{1,0:T(8,128)(2,1)S(1)} %pad_maximum_fusion.1.own), channel_id=1, source_target_pairs={{0,2},{1,3},{2,0},{3,1},{4,6},{5,7},{6,4},{7,5},{8,10},{9,11},{10,... | collective-permute-start | bytes 393224 | tf_op jit(solution)/shard_map/ppermute | solution.py:278
  5.2 0.9 %collective-permute-start.1 = (bf16[256,256]{1,0:T(8,128)(2,1)S(1)}, bf16[256,256]{1,0:T(8,128)(2,1)S(1)}, u32[]{:S(2)}, u32[]{:S(2)}) collective-permute-start(bf16[256,256]{1,0:T(8,128)(2,1)S(1)} %pad_maximum_fusion.1.own), channel_id=1, source_target_pairs={{0,1},{1,2},{2,3},{3,0},{4,5},{5,6},{6,7},{7,4},{8,9},{9,10},{10,1... | collective-permute-start | bytes 393224 | tf_op jit(solution)/shard_map/ppermute | solution.py:278
  6.1 3.9 %collective-permute-start = (bf16[256,256]{1,0:T(8,128)(2,1)S(1)}, bf16[256,256]{1,0:T(8,128)(2,1)S(1)}, u32[]{:S(2)}, u32[]{:S(2)}) collective-permute-start(bf16[256,256]{1,0:T(8,128)(2,1)S(1)} %pad_maximum_fusion.1.own), channel_id=1, source_target_pairs={{0,8},{1,9},{2,10},{3,11},{4,12},{5,13},{6,14},{7,15},{8,0},{9,1},... | collective-permute-start | bytes 393224 | tf_op jit(solution)/shard_map/ppermute | solution.py:284
  10.0 1.0 %copy-done = bf16[256,8,128]{2,1,0:T(8,128)(2,1)S(1)} copy-done((bf16[256,8,128]{2,1,0:T(8,128)(2,1)S(1)}, bf16[256,8,128]{2,1,0:T(8,128)(2,1)}, u32[]{:S(2)}) %copy-start) | copy-done | bytes 524312
  11.0 1.0 %copy-done.1 = bf16[256,8,128]{2,1,0:T(8,128)(2,1)S(1)} copy-done((bf16[256,8,128]{2,1,0:T(8,128)(2,1)S(1)}, bf16[256,8,128]{2,1,0:T(8,128)(2,1)}, u32[]{:S(2)}) %copy-start.1) | copy-done | bytes 524312
  12.1 0.1 load.1
  12.2 0.1 collective-permute-done.2
  12.3 1.4 %collective-permute-done.1 = bf16[256,256]{1,0:T(8,128)(2,1)S(1)} collective-permute-done((bf16[256,256]{1,0:T(8,128)(2,1)S(1)}, bf16[256,256]{1,0:T(8,128)(2,1)S(1)}, u32[]{:S(2)}, u32[]{:S(2)}) %collective-permute-start.1) | collective-permute-done | bytes 131104 | tf_op jit(solution)/shard_map/ppermute | solution.py:278
  13.7 0.0 collective-permute-done.refs_0_
  13.7 0.1 pad_maximum_fusion.refs_0_
  13.8 4.1 %collective-permute-start.8 = (bf16[4,256,256]{2,1,0:T(8,128)(2,1)S(1)}, bf16[4,256,256]{2,1,0:T(8,128)(2,1)S(1)}, u32[]{:S(2)}, u32[]{:S(2)}) collective-permute-start(bf16[4,256,256]{2,1,0:T(8,128)(2,1)S(1)} %pad_maximum_fusion.refs_0_), channel_id=1, source_target_pairs={{0,12},{1,13},{2,14},{3,15},{4,0},{5,1},{6,2},{7,3},{8,4},{9,5},{1... | collective-permute-start | bytes 1572872 | tf_op jit(solution)/shard_map/ppermute | solution.py:284
  17.9 1.4 %collective-permute-start.6 = (bf16[256,256]{1,0:T(8,128)(2,1)S(1)}, bf16[256,256]{1,0:T(8,128)(2,1)S(1)}, u32[]{:S(2)}, u32[]{:S(2)}) collective-permute-start(bf16[256,256]{1,0:T(8,128)(2,1)S(1)} %collective-permute-done.refs_0_), channel_id=1, source_target_pairs={{0,3},{1,0},{2,1},{3,2},{4,7},{5,4},{6,5},{7,6},{8,11},{9,8},{10,9... | collective-permute-start | bytes 393224 | tf_op jit(solution)/shard_map/ppermute | solution.py:278
  19.2 1.5 %collective-permute-start.5 = (bf16[256,256]{1,0:T(8,128)(2,1)S(1)}, bf16[256,256]{1,0:T(8,128)(2,1)S(1)}, u32[]{:S(2)}, u32[]{:S(2)}) collective-permute-start(bf16[256,256]{1,0:T(8,128)(2,1)S(1)} %collective-permute-done.refs_0_), channel_id=1, source_target_pairs={{0,2},{1,3},{2,0},{3,1},{4,6},{5,7},{6,4},{7,5},{8,10},{9,11},{10,... | collective-permute-start | bytes 393224 | tf_op jit(solution)/shard_map/ppermute | solution.py:278
  20.8 1.3 %forward_first.1 = (bf16[4,256,2048]{2,1,0:T(8,128)(2,1)S(1)}, f32[16,2048]{1,0:T(8,128)S(1)}, f32[128,2048]{1,0:T(8,128)S(1)}) custom-call(s32[1]{0:T(128)} %bitcast.3.cnt, bf16[2048,128]{1,0:T(8,128)(2,1)S(1)} %get-tuple-element.59.q, bf16[2048,128]{1,0:T(8,128)(2,1)S(1)} %get-tuple-element.60.go, bf16[4,256,256]{2,1,0:T(8,128)(2,1)S(1)} %pad_maximum_fusion.refs_0_), custom_call_target="tpu_custom_call" | custom-call | flops 1000 | bytes 1000 | tf_op jit(solution)/shard_map/forward_first/pallas_call | solution.py:165
  22.1 2.1 %collective-permute-done.6.refs_3_ = bf16[256,256]{1,0:T(8,128)(2,1)S(1)} collective-permute-done((bf16[256,256]{1,0:T(8,128)(2,1)S(1)}, bf16[256,256]{1,0:T(8,128)(2,1)S(1)}, u32[]{:S(2)}, u32[]{:S(2)}) %collective-permute-start.6) | collective-permute-done | bytes 131104 | tf_op jit(solution)/shard_map/ppermute | solution.py:278
  24.2 2.2 %collective-permute-done.5.refs_2_ = bf16[256,256]{1,0:T(8,128)(2,1)S(1)} collective-permute-done((bf16[256,256]{1,0:T(8,128)(2,1)S(1)}, bf16[256,256]{1,0:T(8,128)(2,1)S(1)}, u32[]{:S(2)}, u32[]{:S(2)}) %collective-permute-start.5) | collective-permute-done | bytes 131104 | tf_op jit(solution)/shard_map/ppermute | solution.py:278
  26.5 1.2 %collective-permute-done.4.refs_1_ = bf16[256,256]{1,0:T(8,128)(2,1)S(1)} collective-permute-done((bf16[256,256]{1,0:T(8,128)(2,1)S(1)}, bf16[256,256]{1,0:T(8,128)(2,1)S(1)}, u32[]{:S(2)}, u32[]{:S(2)}) %collective-permute-start.4) | collective-permute-done | bytes 131104 | tf_op jit(solution)/shard_map/ppermute | solution.py:278
  27.7 0.1 forward.2
  27.8 1.3 %collective-permute-done.8.refs_0_ = bf16[4,256,256]{2,1,0:T(8,128)(2,1)S(1)} collective-permute-done((bf16[4,256,256]{2,1,0:T(8,128)(2,1)S(1)}, bf16[4,256,256]{2,1,0:T(8,128)(2,1)S(1)}, u32[]{:S(2)}, u32[]{:S(2)}) %collective-permute-start.8) | collective-permute-done | bytes 524320 | tf_op jit(solution)/shard_map/ppermute | solution.py:284
  29.1 0.1 forward.3
  29.1 3.3 %collective-permute-done.7.refs_0_ = bf16[4,256,256]{2,1,0:T(8,128)(2,1)S(1)} collective-permute-done((bf16[4,256,256]{2,1,0:T(8,128)(2,1)S(1)}, bf16[4,256,256]{2,1,0:T(8,128)(2,1)S(1)}, u32[]{:S(2)}, u32[]{:S(2)}) %collective-permute-start.7) | collective-permute-done | bytes 524320 | tf_op jit(solution)/shard_map/ppermute | solution.py:284
  32.5 0.4 forward_last.1
  32.9 0.3 backward.3
  33.2 1.3 %collective-permute-start.12 = (bf16[4,256,256]{2,1,0:T(8,128)(2,1)S(1)}, bf16[4,256,256]{2,1,0:T(8,128)(2,1)S(1)}, u32[]{:S(2)}, u32[]{:S(2)}) collective-permute-start(bf16[4,256,256]{2,1,0:T(8,128)(2,1)S(1)} %get-tuple-element.84), channel_id=1, source_target_pairs={{12,0},{13,1},{14,2},{15,3},{28,16},{29,17},{30,18},{31,19},{44,32... | collective-permute-start | bytes 1572872 | tf_op jit(solution)/shard_map/ppermute | solution.py:284
  34.5 0.1 backward.4
  34.6 16.5 %collective-permute-start.13 = (bf16[4,256,256]{2,1,0:T(8,128)(2,1)S(1)}, bf16[4,256,256]{2,1,0:T(8,128)(2,1)S(1)}, u32[]{:S(2)}, u32[]{:S(2)}) collective-permute-start(bf16[4,256,256]{2,1,0:T(8,128)(2,1)S(1)} %get-tuple-element.92), channel_id=1, source_target_pairs={{0,12},{1,13},{2,14},{3,15},{4,0},{5,1},{6,2},{7,3},{8,4},{9,5},{1... | collective-permute-start | bytes 1572872 | tf_op jit(solution)/shard_map/ppermute | solution.py:284
  51.2 0.4 backward.5
  51.5 0.6 collective-permute-start.9
  52.2 1.1 %collective-permute-start.10 = (bf16[256,256]{1,0:T(8,128)(2,1)S(1)}, bf16[256,256]{1,0:T(8,128)(2,1)S(1)}, u32[]{:S(2)}, u32[]{:S(2)}) collective-permute-start(bf16[256,256]{1,0:T(8,128)(2,1)S(1)} %get-tuple-element.80), channel_id=1, source_target_pairs={{0,2},{1,3},{2,0},{3,1},{4,6},{5,7},{6,4},{7,5},{8,10},{9,11},{10,... | collective-permute-start | bytes 393224 | tf_op jit(solution)/shard_map/ppermute | solution.py:278
  53.3 0.9 %collective-permute-start.11 = (bf16[256,256]{1,0:T(8,128)(2,1)S(1)}, bf16[256,256]{1,0:T(8,128)(2,1)S(1)}, u32[]{:S(2)}, u32[]{:S(2)}) collective-permute-start(bf16[256,256]{1,0:T(8,128)(2,1)S(1)} %get-tuple-element.81), channel_id=1, source_target_pairs={{0,1},{1,2},{2,3},{3,0},{4,5},{5,6},{6,7},{7,4},{8,9},{9,10},{10,1... | collective-permute-start | bytes 393224 | tf_op jit(solution)/shard_map/ppermute | solution.py:278
  54.1 2.2 %collective-permute-done.12 = bf16[4,256,256]{2,1,0:T(8,128)(2,1)S(1)} collective-permute-done((bf16[4,256,256]{2,1,0:T(8,128)(2,1)S(1)}, bf16[4,256,256]{2,1,0:T(8,128)(2,1)S(1)}, u32[]{:S(2)}, u32[]{:S(2)}) %collective-permute-start.12) | collective-permute-done | bytes 524320 | tf_op jit(solution)/shard_map/ppermute | solution.py:284
  56.4 1.4 %backward_last.1 = (bf16[256,256]{1,0:T(8,128)(2,1)S(1)}, bf16[256,256]{1,0:T(8,128)(2,1)S(1)}, bf16[256,256]{1,0:T(8,128)(2,1)S(1)}, bf16[256,256]{1,0:T(8,128)(2,1)S(1)}, f32[128,2048]{1,0:T(8,128)S(1)}) custom-call(s32[1]{0:T(128)} %bitcast.3.cnt, bf16[2048,128]{1,0:T(8,128)(2,1)S(1)} %get-tuple-element.59.q, bf16[2048,128]{1,0:T(8,128)(2,1)S(1)} %get-tuple-element.60.go, ...), custom_call_target="tpu_custom_call" | custom-call | flops 1000 | bytes 1000 | tf_op jit(solution)/shard_map/backward_last/pallas_call | solution.py:238
  57.8 0.9 %collective-permute-done.10 = bf16[256,256]{1,0:T(8,128)(2,1)S(1)} collective-permute-done((bf16[256,256]{1,0:T(8,128)(2,1)S(1)}, bf16[256,256]{1,0:T(8,128)(2,1)S(1)}, u32[]{:S(2)}, u32[]{:S(2)}) %collective-permute-start.10) | collective-permute-done | bytes 131104 | tf_op jit(solution)/shard_map/ppermute | solution.py:278
  58.7 1.3 %collective-permute-done.11 = bf16[256,256]{1,0:T(8,128)(2,1)S(1)} collective-permute-done((bf16[256,256]{1,0:T(8,128)(2,1)S(1)}, bf16[256,256]{1,0:T(8,128)(2,1)S(1)}, u32[]{:S(2)}, u32[]{:S(2)}) %collective-permute-start.11) | collective-permute-done | bytes 131104 | tf_op jit(solution)/shard_map/ppermute | solution.py:278
  60.0 0.1 add_convert_fusion
  60.1 1.3 %collective-permute-start.17 = (bf16[256,256]{1,0:T(8,128)(2,1)S(1)}, bf16[256,256]{1,0:T(8,128)(2,1)S(1)}, u32[]{:S(2)}, u32[]{:S(2)}) collective-permute-start(bf16[256,256]{1,0:T(8,128)(2,1)S(1)} %add_convert_fusion), channel_id=1, source_target_pairs={{8,0},{9,1},{10,2},{11,3},{12,4},{13,5},{14,6},{15,7},{24,16},{25,... | collective-permute-start | bytes 393224 | tf_op jit(solution)/shard_map/ppermute | solution.py:284
  61.4 0.2 fusion.4
  61.6 0.1 collective-permute-start.16
  61.7 3.1 %collective-permute-start.15 = (bf16[256,256]{1,0:T(8,128)(2,1)S(1)}, bf16[256,256]{1,0:T(8,128)(2,1)S(1)}, u32[]{:S(2)}, u32[]{:S(2)}) collective-permute-start(bf16[256,256]{1,0:T(8,128)(2,1)S(1)} %get-tuple-element.111), channel_id=1, source_target_pairs={{0,2},{1,3},{2,0},{3,1},{4,6},{5,7},{6,4},{7,5},{8,10},{9,11},{10,... | collective-permute-start | bytes 393224 | tf_op jit(solution)/shard_map/ppermute | solution.py:278
  64.8 1.1 %collective-permute-start.14 = (bf16[256,256]{1,0:T(8,128)(2,1)S(1)}, bf16[256,256]{1,0:T(8,128)(2,1)S(1)}, u32[]{:S(2)}, u32[]{:S(2)}) collective-permute-start(bf16[256,256]{1,0:T(8,128)(2,1)S(1)} %get-tuple-element.112), channel_id=1, source_target_pairs={{0,3},{1,0},{2,1},{3,2},{4,7},{5,4},{6,5},{7,6},{8,11},{9,8},{10,9... | collective-permute-start | bytes 393224 | tf_op jit(solution)/shard_map/ppermute | solution.py:278
  65.9 1.4 %finish.1 = (bf16[2048,128]{1,0:T(8,128)(2,1)}, f32[2048,128]{1,0:T(8,128)}) custom-call(bf16[128,2048]{1,0:T(8,128)(2,1)S(1)} %get-tuple-element.95.att_t, f32[128,2048]{1,0:T(8,128)S(1)} %get-tuple-element.96.dq_t), custom_call_target="tpu_custom_call" | custom-call | flops 1000 | bytes 1000 | tf_op jit(solution)/shard_map/finish/pallas_call | solution.py:257
  67.4 1.1 %collective-permute-done.17 = bf16[256,256]{1,0:T(8,128)(2,1)S(1)} collective-permute-done((bf16[256,256]{1,0:T(8,128)(2,1)S(1)}, bf16[256,256]{1,0:T(8,128)(2,1)S(1)}, u32[]{:S(2)}, u32[]{:S(2)}) %collective-permute-start.17) | collective-permute-done | bytes 131104 | tf_op jit(solution)/shard_map/ppermute | solution.py:284
  68.5 0.8 %collective-permute-done.15 = bf16[256,256]{1,0:T(8,128)(2,1)S(1)} collective-permute-done((bf16[256,256]{1,0:T(8,128)(2,1)S(1)}, bf16[256,256]{1,0:T(8,128)(2,1)S(1)}, u32[]{:S(2)}, u32[]{:S(2)}) %collective-permute-start.15) | collective-permute-done | bytes 131104 | tf_op jit(solution)/shard_map/ppermute | solution.py:278
  69.3 0.9 %collective-permute-done.14 = bf16[256,256]{1,0:T(8,128)(2,1)S(1)} collective-permute-done((bf16[256,256]{1,0:T(8,128)(2,1)S(1)}, bf16[256,256]{1,0:T(8,128)(2,1)S(1)}, u32[]{:S(2)}, u32[]{:S(2)}) %collective-permute-start.14) | collective-permute-done | bytes 131104 | tf_op jit(solution)/shard_map/ppermute | solution.py:278
  70.1 0.1 fusion.3
  70.2 0.7 %fusion.7 = (f32[256,128]{1,0:T(8,128)}, f32[256,128]{1,0:T(8,128)}) fusion(f32[256,256]{1,0:T(8,128)S(1)} %fusion.3), kind=kLoop, calls=%fused_computation.22 | loop fusion | bytes 524288 | tf_op jit(solution)/shard_map/slice | solution.py:327
  (8 shorter events, 0.0 us)
Async XLA Ops:
  1.5 10.6 %collective-permute-start.3 = (bf16[256,256]{1,0:T(8,128)(2,1)S(1)}, bf16[256,256]{1,0:T(8,128)(2,1)S(1)}, u32[]{:S(2)}, u32[]{:S(2)}) collective-permute-start(bf16[256,256]{1,0:T(8,128)(2,1)S(1)} %pad_maximum_fusion.1.own), channel_id=1, source_target_pairs={{0,3},{1,0},{2,1},{3,2},{4,7},{5,4},{6,5},{7,6},{8,11},{9,8},{10,9... | collective-permute-start | bytes 393224 | tf_op jit(solution)/shard_map/ppermute | solution.py:278
  4.4 7.9 %collective-permute-start.2 = (bf16[256,256]{1,0:T(8,128)(2,1)S(1)}, bf16[256,256]{1,0:T(8,128)(2,1)S(1)}, u32[]{:S(2)}, u32[]{:S(2)}) collective-permute-start(bf16[256,256]{1,0:T(8,128)(2,1)S(1)} %pad_maximum_fusion.1.own), channel_id=1, source_target_pairs={{0,2},{1,3},{2,0},{3,1},{4,6},{5,7},{6,4},{7,5},{8,10},{9,11},{10,... | collective-permute-start | bytes 393224 | tf_op jit(solution)/shard_map/ppermute | solution.py:278
  5.2 8.5 %collective-permute-start.1 = (bf16[256,256]{1,0:T(8,128)(2,1)S(1)}, bf16[256,256]{1,0:T(8,128)(2,1)S(1)}, u32[]{:S(2)}, u32[]{:S(2)}) collective-permute-start(bf16[256,256]{1,0:T(8,128)(2,1)S(1)} %pad_maximum_fusion.1.own), channel_id=1, source_target_pairs={{0,1},{1,2},{2,3},{3,0},{4,5},{5,6},{6,7},{7,4},{8,9},{9,10},{10,1... | collective-permute-start | bytes 393224 | tf_op jit(solution)/shard_map/ppermute | solution.py:278
  6.1 7.6 %collective-permute-start = (bf16[256,256]{1,0:T(8,128)(2,1)S(1)}, bf16[256,256]{1,0:T(8,128)(2,1)S(1)}, u32[]{:S(2)}, u32[]{:S(2)}) collective-permute-start(bf16[256,256]{1,0:T(8,128)(2,1)S(1)} %pad_maximum_fusion.1.own), channel_id=1, source_target_pairs={{0,8},{1,9},{2,10},{3,11},{4,12},{5,13},{6,14},{7,15},{8,0},{9,1},... | collective-permute-start | bytes 393224 | tf_op jit(solution)/shard_map/ppermute | solution.py:284
  10.0 1.0 %copy-start = (bf16[256,8,128]{2,1,0:T(8,128)(2,1)S(1)}, bf16[256,8,128]{2,1,0:T(8,128)(2,1)}, u32[]{:S(2)}) copy-start(bf16[256,8,128]{2,1,0:T(8,128)(2,1)} %param.4) | copy-start | bytes 1572868
  11.0 1.0 %copy-start.1 = (bf16[256,8,128]{2,1,0:T(8,128)(2,1)S(1)}, bf16[256,8,128]{2,1,0:T(8,128)(2,1)}, u32[]{:S(2)}) copy-start(bf16[256,8,128]{2,1,0:T(8,128)(2,1)} %param.7) | copy-start | bytes 1572868
  13.8 15.3 %collective-permute-start.8 = (bf16[4,256,256]{2,1,0:T(8,128)(2,1)S(1)}, bf16[4,256,256]{2,1,0:T(8,128)(2,1)S(1)}, u32[]{:S(2)}, u32[]{:S(2)}) collective-permute-start(bf16[4,256,256]{2,1,0:T(8,128)(2,1)S(1)} %pad_maximum_fusion.refs_0_), channel_id=1, source_target_pairs={{0,12},{1,13},{2,14},{3,15},{4,0},{5,1},{6,2},{7,3},{8,4},{9,5},{1... | collective-permute-start | bytes 1572872 | tf_op jit(solution)/shard_map/ppermute | solution.py:284
  17.9 14.6 %collective-permute-start.7 = (bf16[4,256,256]{2,1,0:T(8,128)(2,1)S(1)}, bf16[4,256,256]{2,1,0:T(8,128)(2,1)S(1)}, u32[]{:S(2)}, u32[]{:S(2)}) collective-permute-start(bf16[4,256,256]{2,1,0:T(8,128)(2,1)S(1)} %pad_maximum_fusion.refs_0_), channel_id=1, source_target_pairs={{0,4},{1,5},{2,6},{3,7},{4,8},{5,9},{6,10},{7,11},{8,12},{9,13},{1... | collective-permute-start | bytes 1572872 | tf_op jit(solution)/shard_map/ppermute | solution.py:284
  17.9 6.4 %collective-permute-start.6 = (bf16[256,256]{1,0:T(8,128)(2,1)S(1)}, bf16[256,256]{1,0:T(8,128)(2,1)S(1)}, u32[]{:S(2)}, u32[]{:S(2)}) collective-permute-start(bf16[256,256]{1,0:T(8,128)(2,1)S(1)} %collective-permute-done.refs_0_), channel_id=1, source_target_pairs={{0,3},{1,0},{2,1},{3,2},{4,7},{5,4},{6,5},{7,6},{8,11},{9,8},{10,9... | collective-permute-start | bytes 393224 | tf_op jit(solution)/shard_map/ppermute | solution.py:278
  19.2 7.2 %collective-permute-start.5 = (bf16[256,256]{1,0:T(8,128)(2,1)S(1)}, bf16[256,256]{1,0:T(8,128)(2,1)S(1)}, u32[]{:S(2)}, u32[]{:S(2)}) collective-permute-start(bf16[256,256]{1,0:T(8,128)(2,1)S(1)} %collective-permute-done.refs_0_), channel_id=1, source_target_pairs={{0,2},{1,3},{2,0},{3,1},{4,6},{5,7},{6,4},{7,5},{8,10},{9,11},{10,... | collective-permute-start | bytes 393224 | tf_op jit(solution)/shard_map/ppermute | solution.py:278
  20.8 6.9 %collective-permute-start.4 = (bf16[256,256]{1,0:T(8,128)(2,1)S(1)}, bf16[256,256]{1,0:T(8,128)(2,1)S(1)}, u32[]{:S(2)}, u32[]{:S(2)}) collective-permute-start(bf16[256,256]{1,0:T(8,128)(2,1)S(1)} %collective-permute-done.refs_0_), channel_id=1, source_target_pairs={{0,1},{1,2},{2,3},{3,0},{4,5},{5,6},{6,7},{7,4},{8,9},{9,10},{10,1... | collective-permute-start | bytes 393224 | tf_op jit(solution)/shard_map/ppermute | solution.py:278
  33.2 23.2 %collective-permute-start.12 = (bf16[4,256,256]{2,1,0:T(8,128)(2,1)S(1)}, bf16[4,256,256]{2,1,0:T(8,128)(2,1)S(1)}, u32[]{:S(2)}, u32[]{:S(2)}) collective-permute-start(bf16[4,256,256]{2,1,0:T(8,128)(2,1)S(1)} %get-tuple-element.84), channel_id=1, source_target_pairs={{12,0},{13,1},{14,2},{15,3},{28,16},{29,17},{30,18},{31,19},{44,32... | collective-permute-start | bytes 1572872 | tf_op jit(solution)/shard_map/ppermute | solution.py:284
  34.6 26.8 %collective-permute-start.13 = (bf16[4,256,256]{2,1,0:T(8,128)(2,1)S(1)}, bf16[4,256,256]{2,1,0:T(8,128)(2,1)S(1)}, u32[]{:S(2)}, u32[]{:S(2)}) collective-permute-start(bf16[4,256,256]{2,1,0:T(8,128)(2,1)S(1)} %get-tuple-element.92), channel_id=1, source_target_pairs={{0,12},{1,13},{2,14},{3,15},{4,0},{5,1},{6,2},{7,3},{8,4},{9,5},{1... | collective-permute-start | bytes 1572872 | tf_op jit(solution)/shard_map/ppermute | solution.py:284
  51.5 6.2 %collective-permute-start.9 = (bf16[256,256]{1,0:T(8,128)(2,1)S(1)}, bf16[256,256]{1,0:T(8,128)(2,1)S(1)}, u32[]{:S(2)}, u32[]{:S(2)}) collective-permute-start(bf16[256,256]{1,0:T(8,128)(2,1)S(1)} %get-tuple-element.79), channel_id=1, source_target_pairs={{0,3},{1,0},{2,1},{3,2},{4,7},{5,4},{6,5},{7,6},{8,11},{9,8},{10,9... | collective-permute-start | bytes 393224 | tf_op jit(solution)/shard_map/ppermute | solution.py:278
  52.2 6.5 %collective-permute-start.10 = (bf16[256,256]{1,0:T(8,128)(2,1)S(1)}, bf16[256,256]{1,0:T(8,128)(2,1)S(1)}, u32[]{:S(2)}, u32[]{:S(2)}) collective-permute-start(bf16[256,256]{1,0:T(8,128)(2,1)S(1)} %get-tuple-element.80), channel_id=1, source_target_pairs={{0,2},{1,3},{2,0},{3,1},{4,6},{5,7},{6,4},{7,5},{8,10},{9,11},{10,... | collective-permute-start | bytes 393224 | tf_op jit(solution)/shard_map/ppermute | solution.py:278
  53.3 6.8 %collective-permute-start.11 = (bf16[256,256]{1,0:T(8,128)(2,1)S(1)}, bf16[256,256]{1,0:T(8,128)(2,1)S(1)}, u32[]{:S(2)}, u32[]{:S(2)}) collective-permute-start(bf16[256,256]{1,0:T(8,128)(2,1)S(1)} %get-tuple-element.81), channel_id=1, source_target_pairs={{0,1},{1,2},{2,3},{3,0},{4,5},{5,6},{6,7},{7,4},{8,9},{9,10},{10,1... | collective-permute-start | bytes 393224 | tf_op jit(solution)/shard_map/ppermute | solution.py:278
  60.1 8.4 %collective-permute-start.17 = (bf16[256,256]{1,0:T(8,128)(2,1)S(1)}, bf16[256,256]{1,0:T(8,128)(2,1)S(1)}, u32[]{:S(2)}, u32[]{:S(2)}) collective-permute-start(bf16[256,256]{1,0:T(8,128)(2,1)S(1)} %add_convert_fusion), channel_id=1, source_target_pairs={{8,0},{9,1},{10,2},{11,3},{12,4},{13,5},{14,6},{15,7},{24,16},{25,... | collective-permute-start | bytes 393224 | tf_op jit(solution)/shard_map/ppermute | solution.py:284
  61.6 6.9 %collective-permute-start.16 = (bf16[256,256]{1,0:T(8,128)(2,1)S(1)}, bf16[256,256]{1,0:T(8,128)(2,1)S(1)}, u32[]{:S(2)}, u32[]{:S(2)}) collective-permute-start(bf16[256,256]{1,0:T(8,128)(2,1)S(1)} %get-tuple-element.110), channel_id=1, source_target_pairs={{0,1},{1,2},{2,3},{3,0},{4,5},{5,6},{6,7},{7,4},{8,9},{9,10},{10,1... | collective-permute-start | bytes 393224 | tf_op jit(solution)/shard_map/ppermute | solution.py:278
  61.7 7.5 %collective-permute-start.15 = (bf16[256,256]{1,0:T(8,128)(2,1)S(1)}, bf16[256,256]{1,0:T(8,128)(2,1)S(1)}, u32[]{:S(2)}, u32[]{:S(2)}) collective-permute-start(bf16[256,256]{1,0:T(8,128)(2,1)S(1)} %get-tuple-element.111), channel_id=1, source_target_pairs={{0,2},{1,3},{2,0},{3,1},{4,6},{5,7},{6,4},{7,5},{8,10},{9,11},{10,... | collective-permute-start | bytes 393224 | tf_op jit(solution)/shard_map/ppermute | solution.py:278
  64.8 5.3 %collective-permute-start.14 = (bf16[256,256]{1,0:T(8,128)(2,1)S(1)}, bf16[256,256]{1,0:T(8,128)(2,1)S(1)}, u32[]{:S(2)}, u32[]{:S(2)}) collective-permute-start(bf16[256,256]{1,0:T(8,128)(2,1)S(1)} %get-tuple-element.112), channel_id=1, source_target_pairs={{0,3},{1,0},{2,1},{3,2},{4,7},{5,4},{6,5},{7,6},{8,11},{9,8},{10,9... | collective-permute-start | bytes 393224 | tf_op jit(solution)/shard_map/ppermute | solution.py:278
